TPU v7x, 32 devices: a whole 2x2x4 slice. The times are simulated.
32 devices in a mesh: tm: 4 (over z), rows: 8 (over y, x, core).
Axes of the slice: x: 2, y: 2, z: 4, core: 2. Of those that a mesh axis runs over, the one named last changes fastest.
Arguments:
- video: bfloat16 [1, 16, 64, 128, 256], P(None, 'tm', 'rows'), may hold values from -6 to 6
- spatial_weight: bfloat16 [2304, 256], P(('tm', 'rows')), may hold values from -0.125 to 0.125
- temporal_weight: bfloat16 [768, 256], P(('tm', 'rows')), may hold values from -0.21875 to 0.21875
- cotangent: bfloat16 [1, 16, 64, 128, 256], P(None, 'tm', 'rows'), may hold values from -6 to 6
Outputs:
- output: bfloat16 [1, 16, 64, 128, 256], P(None, 'tm', 'rows')
- grad_video: bfloat16 [1, 16, 64, 128, 256], P(None, 'tm', 'rows')
- grad_spatial: float32 [2304, 256], P(('tm', 'rows'))
- grad_temporal: float32 [768, 256], P(('tm', 'rows'))
All inputs are finite; a program needn't handle non-finite values.
Results may differ from a plain program's by a relative error of at most 0.0053.
Values may be sent and summed in bfloat16 or wider, within the bound.
A program may use at most 128 MiB of HBM per device.

v0:
```python
import jax
import jax.numpy as jnp
from jax import lax
from jax.sharding import PartitionSpec as P

epsilon = 1e-06


def with_halo(x, sides, width):
    for axis, dim in sides:
        count, length = (lax.axis_size(axis), x.shape[dim])
        up = [(i, (i + 1) % count) for i in range(count - 1)]
        down = [(j, i) for i, j in up]
        last = lax.slice_in_dim(x, length - width, length, axis=dim)
        leading = lax.slice_in_dim(x, 0, width, axis=dim)
        before = lax.ppermute(last, axis, up)
        after = lax.ppermute(leading, axis, down)
        x = jnp.concatenate([before, x, after], axis=dim)
    return x


def passed_along(x, axis, by):
    count = lax.axis_size(axis)
    pairs = [(i, i + by) for i in range(count) if 0 <= i + by < count]
    return lax.ppermute(x, axis, pairs)


def rim_pad(field):
    rimmed = with_halo(field, (("rows", 2),), 1)
    return jnp.pad(rimmed, ((0, 0), (0, 0), (0, 0), (1, 1), (0, 0)))


def shifted_view(padded, tap_row, tap_col, n_rows, n_cols):
    chans = padded.shape[-1]
    return padded[:, :, tap_row : tap_row + n_rows, tap_col : tap_col + n_cols].reshape(-1, chans)


def conv_three(padded, weight, n_rows, n_cols):
    chans = padded.shape[-1]
    total = None
    for tap_row in range(3):
        for tap_col in range(3):
            block = weight[(3 * tap_row + tap_col) * chans : (3 * tap_row + tap_col + 1) * chans]
            term = jnp.dot(
                shifted_view(padded, tap_row, tap_col, n_rows, n_cols),
                block,
                preferred_element_type=jnp.float32,
            )
            total = term if total is None else total + term
    return total


def kernel_grad(padded, grad_flat, n_rows, n_cols):
    blocks = [
        contract(shifted_view(padded, tap_row, tap_col, n_rows, n_cols), grad_flat)
        for tap_row in range(3)
        for tap_col in range(3)
    ]
    return jnp.concatenate(blocks, axis=0)


def frame_cols(padded, n_frames):
    chans = padded.shape[-1]
    return jnp.concatenate([padded[:, k : k + n_frames] for k in range(3)], axis=-1).reshape(
        -1, 3 * chans
    )


def silu_slope(value):
    sigmoid = jax.nn.sigmoid(value)
    return sigmoid * (1.0 + value * (1.0 - sigmoid))


def contract(left, right):
    return lax.dot_general(
        left, right, (((0,), (0,)), ((), ())), preferred_element_type=jnp.float32
    )


def reverse_spatial(weight, chans):
    return (
        weight.reshape(3, 3, chans, chans)[::-1, ::-1]
        .transpose(0, 1, 3, 2)
        .reshape(9 * chans, chans)
    )


def reverse_temporal(weight, chans):
    return weight.reshape(3, chans, chans)[::-1].transpose(0, 2, 1).reshape(3 * chans, chans)


def shards(video, spatial_weight, temporal_weight, cotangent):
    n_batch, n_frames, n_rows, n_cols, chans = video.shape
    full_spatial, full_temporal = (
        lax.all_gather(spatial_weight, ("tm", "rows"), axis=0, tiled=True),
        lax.all_gather(temporal_weight, ("tm", "rows"), axis=0, tiled=True),
    )
    values = video.astype(jnp.float32)
    inv_rms = lax.rsqrt(jnp.mean(values * values, axis=-1, keepdims=True) + epsilon)
    normed = values * inv_rms
    activated = jax.nn.silu(normed).astype(jnp.bfloat16)
    padded_act = rim_pad(activated)
    pre_act = conv_three(padded_act, full_spatial, n_rows, n_cols).reshape(video.shape)
    hidden = jax.nn.silu(pre_act).astype(jnp.bfloat16)
    back_temporal = reverse_temporal(full_temporal, chans)
    past = passed_along(hidden[:, n_frames - 2 :], "tm", 1)
    ahead = passed_along(cotangent[:, :2], "tm", -1)
    from_past = frame_cols(jnp.concatenate([past, hidden], axis=1), n_frames)
    from_ahead = frame_cols(jnp.concatenate([cotangent, ahead], axis=1), n_frames)
    mixed = jnp.dot(from_past, full_temporal, preferred_element_type=jnp.float32).reshape(
        video.shape
    )
    back = jnp.dot(from_ahead, back_temporal, preferred_element_type=jnp.float32).reshape(
        video.shape
    )
    grad_temporal = contract(from_past, cotangent.reshape(-1, chans))
    output = (values + mixed).astype(jnp.bfloat16)
    grad_pre = (back * silu_slope(pre_act)).astype(jnp.bfloat16)
    grad_spatial = kernel_grad(padded_act, grad_pre.reshape(-1, chans), n_rows, n_cols)
    back_spatial = reverse_spatial(full_spatial, chans)
    grad_act = conv_three(rim_pad(grad_pre), back_spatial, n_rows, n_cols).reshape(video.shape)
    grad_norm = grad_act * silu_slope(normed)
    grad_in = inv_rms * (grad_norm - normed * jnp.mean(grad_norm * normed, axis=-1, keepdims=True))
    grad_video = (cotangent.astype(jnp.float32) + grad_in).astype(jnp.bfloat16)
    first_spatial, first_temporal = (
        lax.psum_scatter(grad_spatial, "tm", scatter_dimension=0, tiled=True),
        lax.psum_scatter(grad_temporal, "tm", scatter_dimension=0, tiled=True),
    )
    spatial_part, temporal_part = (
        lax.psum_scatter(first_spatial, "rows", scatter_dimension=0, tiled=True),
        lax.psum_scatter(first_temporal, "rows", scatter_dimension=0, tiled=True),
    )
    total_cells = n_batch * n_frames * n_rows * n_cols * lax.axis_size("tm") * lax.axis_size("rows")
    factor = float(total_cells) ** (-0.5)
    return (output, grad_video, spatial_part * factor, temporal_part * factor)


def solution(mesh):
    in_specs = (
        P(None, "tm", "rows", None, None),
        P(("tm", "rows"), None),
        P(("tm", "rows"), None),
        P(None, "tm", "rows", None, None),
    )
    out_specs = (
        P(None, "tm", "rows", None, None),
        P(None, "tm", "rows", None, None),
        P(("tm", "rows"), None),
        P(("tm", "rows"), None),
    )
    return jax.shard_map(shards, mesh=mesh, in_specs=in_specs, out_specs=out_specs, check_vma=False)
```

profile of v0, /device:TPU:0, one launch (start us, length us, event | category | flops | bytes accessed | tf_op | source)
XLA Modules:
  0.0 305.2 jit_solution(11006406845352237332)
XLA Ops:
  7.2 2.4 fusion.30
  11.8 3.0 collective-permute-start
  16.2 2.3 slice.175
  19.9 62.7 %all_gather.7 = bf16[768,256]{1,0:T(8,128)(2,1)S(1)} all-gather(bf16[24,256]{1,0:T(8,128)(2,1)S(1)} %copy-done.29), channel_id=1, replica_groups=mesh['tm'=4,'rows'=8] {'tm','rows'}, dimensions={0}, use_global_device_ids=true | all-gather | bytes 405504 | tf_op jit(solution)/shard_map/all_gather | solution.py:96
  84.2 1.7 constant_dynamic-update-slice_fusion.1
  86.0 3.4 %pad_maximum_fusion.3 = (bf16[1,4,8,128,256]{4,3,2,1,0:T(8,128)(2,1)}, bf16[1,4,8,128,256]{4,3,2,1,0:T(8,128)(2,1)}) fusion(bf16[1,4,1,128,256]{4,3,2,1,0:T(8,128)(2,1)} %collective-permute-done.1, bf16[1,4,8,128,256]{4,3,2,1,0:T(8,128)(2,1)S(1)} %fusion.21, bf16[1,4,1,128,256]{4,3,2,1,0:T(8,128)(2,1)} %collective-permute-done), kind=kLoop, calls=%fused_computation.68 | loop fusion | flops 2097152 | bytes 6815744 | tf_op jit(solution)/shard_map/concatenate | solution.py:18
  89.3 2.3 select_maximum_fusion.2
  91.7 5.4 %fusion.146 = (bf16[1,4,8,128,256]{4,3,2,1,0:T(8,128)(2,1)}, bf16[1,4,8,128,256]{4,3,2,1,0:T(8,128)(2,1)}, bf16[1,4,8,128,256]{4,3,2,1,0:T(8,128)(2,1)}, bf16[1,...) fusion(bf16[1,4,10,130,256]{4,3,2,1,0:T(8,128)(2,1)S(1)} %select_maximu, ...), kind=kLoop, calls=%fused_computation.150 | loop fusion | bytes 25165824 | tf_op jit(solution)/shard_map/slice | solution.py:35
  97.2 2.5 fusion.144
  99.7 2.5 fusion.133
  112.5 2.8 multiply_convert_fusion.1
  117.6 2.5 collective-permute-start.2
  120.1 2.7 multiply_convert_fusion
  122.8 1.5 fusion.61
  126.5 2.1 collective-permute-start.4
  130.0 1.5 copy.31
  131.5 3.2 %fusion.73 = f32[2304,256]{1,0:T(8,128)} fusion(f32[2304,256]{1,0:T(8,128)} %fusion.67, bf16[4,8,128,256]{3,2,1,0:T(8,128)(2,1)S(1)} %multiply_convert_fusion, bf16[1,4,10,130,256]{4,3,2,1,0:T(8,128)(2,1)} %copy-done), kind=kOutput, calls=%fused_computation.96 | convolution fusion | flops 536870912 | bytes 4456448 | tf_op jit(solution)/shard_map/dot_general | solution.py:75
  136.4 1.5 fusion.85
  137.8 4.6 %collective-permute-done.2 = bf16[1,2,8,128,256]{4,3,2,1,0:T(8,128)(2,1)} collective-permute-done((bf16[1,2,8,128,256]{4,3,2,1,0:T(8,128)(2,1)}, bf16[1,2,8,128,256]{4,3,2,1,0:T(8,128)(2,1)}, u32[]{:S(2)}, u32[]{:S(2)}) %collective-permute-start.2) | collective-permute-done | bytes 1048608 | tf_op jit(solution)/shard_map/ppermute | solution.py:25
  145.1 3.7 %fusion.55 = f32[768,256]{1,0:T(8,128)} fusion(bf16[1,4,8,128,256]{4,3,2,1,0:T(8,128)(2,1)S(1)} %copy-done.12, bf16[1,4,8,128,256]{4,3,2,1,0:T(8,128)(2,1)S(1)} %copy-done.14, bf16[1,2,8,128,256]{4,3,2,1,0:T(8,128)(2,1)} %collective-permute-done.2, bf16[1,4,8,128,256]{4,3,2,1,0:T(8,128)(2,1)S(1)} %fusion.35), kind=kOutput, calls=%fused_computation.89 | convolution fusion | flops 1635778560 | bytes 8126464 | tf_op jit(solution)/shard_map/dot_general | solution.py:75
  149.0 3.2 %fusion.91 = f32[2304,256]{1,0:T(8,128)} fusion(f32[2304,256]{1,0:T(8,128)} %fusion.85, bf16[4,8,128,256]{3,2,1,0:T(8,128)(2,1)S(1)} %multiply_convert_fusion, bf16[1,4,10,130,256]{4,3,2,1,0:T(8,128)(2,1)} %copy-done), kind=kOutput, calls=%fused_computation.102 | convolution fusion | flops 536870912 | bytes 4456448 | tf_op jit(solution)/shard_map/dot_general | solution.py:75
  153.8 1.5 fusion.103
  155.3 1.5 fusion.109
  157.1 2.3 select_maximum_fusion
  159.4 5.2 %fusion.145 = (bf16[1,4,8,128,256]{4,3,2,1,0:T(8,128)(2,1)S(1)}, bf16[1,4,8,128,256]{4,3,2,1,0:T(8,128)(2,1)S(1)}, bf16[1,4,8,128,256]{4,3,2,1,0:T(8,128)(2,1)S(...) fusion(bf16[1,4,10,130,256]{4,3,2,1,0:T(8,128)(2,1)S(1)} %selec, ...), kind=kLoop, calls=%fused_computation.149 | loop fusion | bytes 25165824 | tf_op jit(solution)/shard_map/slice | solution.py:35
  173.2 2.3 fusion.25
  175.9 5.5 %fusion.29 = bf16[1,4,8,128,256]{4,3,2,1,0:T(8,128)(2,1)} fusion(bf16[1,4,8,128,256]{4,3,2,1,0:T(8,128)(2,1)S(1)} %copy-done.8, bf16[1,4,8,128,256]{4,3,2,1,0:T(8,128)(2,1)} %param.7, f32[4,8,128]{2,1,0:T(8,128)S(1)} %broadcast_multiply_fusion.2, f32[4,8,128]{2,1,0:T(8,128)S(1)} %add_rsqrt_fusion, f32[4096,256]{1,0:T(8,128)} %copy-done.6), kind=kLoop, calls=%fused_computation.52 | loop fusion | flops 16777216 | bytes 10518528 | tf_op jit(solution)/shard_map/convert_element_type | solution.py:124
  181.4 42.0 %reduce-scatter.5.cloned.1.call-done = f32[576,256]{1,0:T(8,128)} async-done(((f32[2304,256]{1,0:T(8,128)}), f32[576,256]{1,0:T(8,128)}) %reduce-scatter.5.cloned.1.call-update) | async-done | bytes 589840 | tf_op jit(solution)/shard_map/reduce_scatter | solution.py:126
  223.5 4.8 %fusion.31 = bf16[1,4,8,128,256]{4,3,2,1,0:T(8,128)(2,1)} fusion(bf16[1,4,8,128,256]{4,3,2,1,0:T(8,128)(2,1)S(1)} %copy-done.8, bf16[1,4,8,128,256]{4,3,2,1,0:T(8,128)(2,1)} %bitcast.248, bf16[1,4,8,128,256]{4,3,2,1,0:T(8,128)(2,1)} %copy-done.13, bf16[1,2,8,128,256]{4,3,2,1,0:T(8,128)(2,1)} %collective-permute-done.2, ...), kind=kOutput, calls=%fused_computation.54 | convolution fusion | flops 1638924288 | bytes 11927552 | tf_op jit(solution)/shard_map/dot_general | solution.py:110
  228.3 31.1 %reduce-scatter.11.cloned.1.call-done = f32[24,256]{1,0:T(8,128)} async-done(((f32[192,256]{1,0:T(8,128)}), f32[24,256]{1,0:T(8,128)}) %reduce-scatter.11.cloned.1.call-update) | async-done | bytes 24592 | tf_op jit(solution)/shard_map/reduce_scatter | solution.py:131
  260.8 36.4 %reduce-scatter.7.cloned.1.call-done = f32[72,256]{1,0:T(8,128)} async-done(((f32[576,256]{1,0:T(8,128)}), f32[72,256]{1,0:T(8,128)}) %reduce-scatter.7.cloned.1.call-update) | async-done | bytes 73744 | tf_op jit(solution)/shard_map/reduce_scatter | solution.py:130
  297.1 1.5 broadcast_multiply_fusion
  (113 shorter events, 39.4 us)
Async XLA Ops:
  7.2 92.5 %all-gather.2.cloned.1.call-start = ((), (), s32[]{:S(2)}) async-start(), calls=%async_computation.4 | async-start | bytes 1216512 | tf_op jit(solution)/shard_map/all_gather | solution.py:95
  7.2 2.4 copy-start.7
  10.9 96.9 %copy-start.4 = (bf16[1,4,8,128,256]{4,3,2,1,0:T(8,128)(2,1)}, bf16[1,4,8,128,256]{4,3,2,1,0:T(8,128)(2,1)S(1)}, u32[]{:S(2)}) copy-start(bf16[1,4,8,128,256]{4,3,2,1,0:T(8,128)(2,1)S(1)} %fusion.21) | copy-start | bytes 6291460
  10.9 8.9 %copy-start.29 = (bf16[24,256]{1,0:T(8,128)(2,1)S(1)}, bf16[24,256]{1,0:T(8,128)(2,1)}, u32[]{:S(2)}) copy-start(bf16[24,256]{1,0:T(8,128)(2,1)} %param.6) | copy-start | bytes 36868
  11.8 74.1 %collective-permute-start = (bf16[1,4,1,128,256]{4,3,2,1,0:T(8,128)(2,1)}, bf16[1,4,1,128,256]{4,3,2,1,0:T(8,128)(2,1)}, u32[]{:S(2)}, u32[]{:S(2)}) collective-permute-start(bf16[1,4,1,128,256]{4,3,2,1,0:T(8,128)(2,1)} %get-tuple-element.24), channel_id=1, source_target_pairs={{0,1},{1,2},{2,3},{3,4},{4,5},{5,6},{6,7},{8,9},{9,10},{10,11},{11... | collective-permute-start | bytes 786440 | tf_op jit(solution)/shard_map/ppermute | solution.py:16
  14.9 71.1 %collective-permute-start.1 = (bf16[1,4,1,128,256]{4,3,2,1,0:T(8,128)(2,1)}, bf16[1,4,1,128,256]{4,3,2,1,0:T(8,128)(2,1)}, u32[]{:S(2)}, u32[]{:S(2)}) collective-permute-start(bf16[1,4,1,128,256]{4,3,2,1,0:T(8,128)(2,1)} %get-tuple-element.25), channel_id=1, source_target_pairs={{1,0},{2,1},{3,2},{4,3},{5,4},{6,5},{7,6},{9,8},{10,9},{11,10},{12... | collective-permute-start | bytes 786440 | tf_op jit(solution)/shard_map/ppermute | solution.py:17
  16.2 159.4 %reduce-scatter.9.cloned.1.call-start = ((), (), s32[]{:S(2)}) async-start(), calls=%async_computation.7 | async-start | bytes 983040 | tf_op jit(solution)/shard_map/reduce_scatter | solution.py:127
  18.6 78.5 %collective-permute-start.3 = (bf16[1,2,8,128,256]{4,3,2,1,0:T(8,128)(2,1)}, bf16[1,2,8,128,256]{4,3,2,1,0:T(8,128)(2,1)S(1)}, u32[]{:S(2)}, u32[]{:S(2)}) collective-permute-start(bf16[1,2,8,128,256]{4,3,2,1,0:T(8,128)(2,1)} %slice.175), channel_id=1, source_target_pairs={{8,0},{16,8},{24,16},{9,1},{17,9},{25,17},{10,2},{18,10},{26,18},{... | collective-permute-start | bytes 3145736 | tf_op jit(solution)/shard_map/ppermute | solution.py:25
  91.7 5.4 %copy-start = (bf16[1,4,10,130,256]{4,3,2,1,0:T(8,128)(2,1)}, bf16[1,4,10,130,256]{4,3,2,1,0:T(8,128)(2,1)S(1)}, u32[]{:S(2)}) copy-start(bf16[1,4,10,130,256]{4,3,2,1,0:T(8,128)(2,1)S(1)} %select_maximum_fusion.2) | copy-start | bytes 7987204
  99.7 2.5 copy-start.10
  99.7 2.6 copy-start.22
  107.8 1.6 copy-start.18
  115.3 4.8 %copy-start.11 = (bf16[1,4,8,128,256]{4,3,2,1,0:T(8,128)(2,1)S(1)}, bf16[1,4,8,128,256]{4,3,2,1,0:T(8,128)(2,1)}, u32[]{:S(2)}) copy-start(bf16[1,4,8,128,256]{4,3,2,1,0:T(8,128)(2,1)} %param.7) | copy-start | bytes 6291460
  115.3 4.8 %copy-start.24 = (bf16[1,4,8,128,256]{4,3,2,1,0:T(8,128)(2,1)S(1)}, bf16[1,4,8,128,256]{4,3,2,1,0:T(8,128)(2,1)}, u32[]{:S(2)}) copy-start(bf16[1,4,8,128,256]{4,3,2,1,0:T(8,128)(2,1)} %get-tuple-element.4) | copy-start | bytes 6291460
  115.3 4.8 %copy-start.25 = (bf16[1,4,8,128,256]{4,3,2,1,0:T(8,128)(2,1)S(1)}, bf16[1,4,8,128,256]{4,3,2,1,0:T(8,128)(2,1)}, u32[]{:S(2)}) copy-start(bf16[1,4,8,128,256]{4,3,2,1,0:T(8,128)(2,1)} %get-tuple-element.5) | copy-start | bytes 6291460
  115.3 4.8 %copy-start.28 = (bf16[3,256,256]{2,1,0:T(8,128)(2,1)S(1)}, bf16[3,256,256]{2,1,0:T(8,128)(2,1)}, u32[]{:S(2)}) copy-start(bf16[3,256,256]{2,1,0:T(8,128)(2,1)} %copy.30) | copy-start | bytes 1179652
  116.5 3.6 %copy-start.13 = (bf16[1,4,8,128,256]{4,3,2,1,0:T(8,128)(2,1)}, bf16[1,4,8,128,256]{4,3,2,1,0:T(8,128)(2,1)S(1)}, u32[]{:S(2)}) copy-start(bf16[1,4,8,128,256]{4,3,2,1,0:T(8,128)(2,1)S(1)} %multiply_convert_fusion.2) | copy-start | bytes 6291460
  117.6 24.9 %collective-permute-start.2 = (bf16[1,2,8,128,256]{4,3,2,1,0:T(8,128)(2,1)}, bf16[1,2,8,128,256]{4,3,2,1,0:T(8,128)(2,1)}, u32[]{:S(2)}, u32[]{:S(2)}) collective-permute-start(bf16[1,2,8,128,256]{4,3,2,1,0:T(8,128)(2,1)} %slice.214), channel_id=1, source_target_pairs={{0,8},{8,16},{16,24},{1,9},{9,17},{17,25},{2,10},{10,18},{18,26},{... | collective-permute-start | bytes 3145736 | tf_op jit(solution)/shard_map/ppermute | solution.py:25
  120.1 2.7 copy-start.1
  126.5 30.5 %collective-permute-start.4 = (bf16[1,4,1,128,256]{4,3,2,1,0:T(8,128)(2,1)}, bf16[1,4,1,128,256]{4,3,2,1,0:T(8,128)(2,1)S(1)}, u32[]{:S(2)}, u32[]{:S(2)}) collective-permute-start(bf16[1,4,1,128,256]{4,3,2,1,0:T(8,128)(2,1)} %get-tuple-element.20), channel_id=1, source_target_pairs={{0,1},{1,2},{2,3},{3,4},{4,5},{5,6},{6,7},{8,9},{9,10},{10,11},{11... | collective-permute-start | bytes 786440 | tf_op jit(solution)/shard_map/ppermute | solution.py:16
  128.6 28.4 %collective-permute-start.5 = (bf16[1,4,1,128,256]{4,3,2,1,0:T(8,128)(2,1)}, bf16[1,4,1,128,256]{4,3,2,1,0:T(8,128)(2,1)}, u32[]{:S(2)}, u32[]{:S(2)}) collective-permute-start(bf16[1,4,1,128,256]{4,3,2,1,0:T(8,128)(2,1)} %get-tuple-element.21), channel_id=1, source_target_pairs={{1,0},{2,1},{3,2},{4,3},{5,4},{6,5},{7,6},{9,8},{10,9},{11,10},{12... | collective-permute-start | bytes 786440 | tf_op jit(solution)/shard_map/ppermute | solution.py:17
  131.5 3.3 %copy-start.2 = (bf16[1,4,10,130,256]{4,3,2,1,0:T(8,128)(2,1)S(1)}, bf16[1,4,10,130,256]{4,3,2,1,0:T(8,128)(2,1)}, u32[]{:S(2)}) copy-start(bf16[1,4,10,130,256]{4,3,2,1,0:T(8,128)(2,1)} %copy-done) | copy-start | bytes 7987204
  136.4 6.0 %copy-start.14 = (bf16[1,4,8,128,256]{4,3,2,1,0:T(8,128)(2,1)S(1)}, bf16[1,4,8,128,256]{4,3,2,1,0:T(8,128)(2,1)}, u32[]{:S(2)}) copy-start(bf16[1,4,8,128,256]{4,3,2,1,0:T(8,128)(2,1)} %copy-done.13) | copy-start | bytes 6291460
  137.8 7.3 %copy-start.12 = (bf16[1,4,8,128,256]{4,3,2,1,0:T(8,128)(2,1)S(1)}, bf16[1,4,8,128,256]{4,3,2,1,0:T(8,128)(2,1)}, u32[]{:S(2)}) copy-start(bf16[1,4,8,128,256]{4,3,2,1,0:T(8,128)(2,1)} %param.7) | copy-start | bytes 6291460
  148.9 74.5 %reduce-scatter.5.cloned.1.call-start = ((), (), s32[]{:S(2)}) async-start(), calls=%async_computation.5 | async-start | bytes 2949120 | tf_op jit(solution)/shard_map/reduce_scatter | solution.py:126
  149.0 3.2 %copy-start.3 = (bf16[1,4,10,130,256]{4,3,2,1,0:T(8,128)(2,1)S(1)}, bf16[1,4,10,130,256]{4,3,2,1,0:T(8,128)(2,1)}, u32[]{:S(2)}) copy-start(bf16[1,4,10,130,256]{4,3,2,1,0:T(8,128)(2,1)} %copy-done) | copy-start | bytes 7987204
  156.8 102.6 %reduce-scatter.11.cloned.1.call-start = ((), (), s32[]{:S(2)}) async-start(), calls=%async_computation.8 | async-start | bytes 221184 | tf_op jit(solution)/shard_map/reduce_scatter | solution.py:131
  159.4 5.2 %copy-start.21 = (bf16[3,3,256,256]{3,2,1,0:T(8,128)(2,1)S(1)}, bf16[3,3,256,256]{3,2,1,0:T(8,128)(2,1)}, u32[]{:S(2)}) copy-start(bf16[3,3,256,256]{3,2,1,0:T(8,128)(2,1)} %copy.31) | copy-start | bytes 3538948
  171.6 1.6 copy-start.8
  172.3 3.2 %copy-start.6 = (f32[4096,256]{1,0:T(8,128)}, f32[4096,256]{1,0:T(8,128)S(1)}, u32[]{:S(2)}) copy-start(f32[4096,256]{1,0:T(8,128)S(1)} %fusion.16) | copy-start | bytes 12582916
  175.6 47.8 %copy-start.27 = (bf16[768,256]{1,0:T(8,128)(2,1)S(1)}, bf16[768,256]{1,0:T(8,128)(2,1)}, u32[]{:S(2)}) copy-start(bf16[768,256]{1,0:T(8,128)(2,1)} %copy-done.26) | copy-start | bytes 1179652
  175.6 121.5 %reduce-scatter.7.cloned.1.call-start = ((), (), s32[]{:S(2)}) async-start(), calls=%async_computation.6 | async-start | bytes 663552 | tf_op jit(solution)/shard_map/reduce_scatter | solution.py:130
  (9 other events, 13.2 us)
Sparse Core Ops, SparseCore 0:
  16.3 58.3 all-gather.1
  149.0 24.7 reduce-scatter.8
  176.1 47.2 reduce-scatter.4
  226.3 33.0 reduce-scatter.10
  262.7 34.3 reduce-scatter.6
where the time goes:
time: 306 us; the launch traced here: 305 us
  waiting for transfers between devices  114 us (37%)
  blocking collectives  62.7 us (20%)
  matrix products  44.7 us (15%)
  local copies, waits for them, and re-layouts  31.1 us (10%)
  other arithmetic  26.1 us (9%)
  between operations  14.3 us (5%)
  starting transfers between devices  12.2 us (4%)
    all_gather x1, blocking collectives, shards(): lax.all_gather(temporal_weight, ('tm', 'rows'), axis=0, tiled=True)  62.7 us
    reduce_scatter x1, waiting for transfers between devices, shards(): lax.psum_scatter(grad_spatial, 'tm', scatter_dimension=0, tiled=True)  42 us
    reduce_scatter x1, waiting for transfers between devices, shards(): lax.psum_scatter(first_spatial, 'rows', scatter_dimension=0, tiled=True)  36.4 us
    reduce_scatter x1, waiting for transfers between devices, shards(): lax.psum_scatter(first_temporal, 'rows', scatter_dimension=0, tiled=True)  31.1 us
    dot_general x10, matrix products, contract(): lax.dot_general(left, right, (((0,), (0,)), ((), ())), preferred_element_...  20.4 us
    dot_general x18, matrix products, conv_three(): jnp.dot(shifted_view(padded, tap_row, tap_col, n_rows, n_cols), block, pr...  16.7 us
    slice x2, local copies, waits for them, and re-layouts, shifted_view(): padded[:, :, tap_row:tap_row + n_rows, tap_col:tap_col + n_cols]  10.6 us
    unnamed x61, local copies, waits for them, and re-layouts  10.2 us
  transfers between devices with their start and end apart: 11, of which 4 were waited for; matrix products, arithmetic and copies ran while one was open for 25% of the time, Pallas kernels for 0%

commit v1 on v0

v1 whole, which is shorter than its diff:
```python
import functools

import jax
import jax.numpy as jnp
from jax import lax
from jax.experimental import pallas as pl
from jax.experimental.pallas import tpu as pltpu
from jax.sharding import PartitionSpec as P

epsilon = 1e-06
MESH = pl.DeviceIdType.MESH
f32 = jnp.float32
bf16 = jnp.bfloat16


def mm(a, b):
    return lax.dot_general(a, b, (((1,), (0,)), ((), ())), preferred_element_type=f32)


def silu_slope(value):
    sigmoid = jax.nn.sigmoid(value)
    return sigmoid * (1.0 + value * (1.0 - sigmoid))


def normalize(values):
    inv_rms = lax.rsqrt(jnp.mean(values * values, axis=-1, keepdims=True) + epsilon)
    return values * inv_rms, inv_rms


def kernel(
    dims, video, shard, cot_hbm, output, grad_video, grads,
    wide, act_t, slope, hid, hid_t, cot, acc_s, acc_t, work, w_s, w_t, wb_s, wb_t, gather,
    edge_out, edge_in, rs_out, rs_in, z_out, z_in,
    ag_z_send, ag_z_recv, ag_send, ag_recv, edge_send, edge_recv, frame_send, frame_recv,
    rs_send, rs_recv, z_send, z_recv, cot_sem,
):
    n_t, n_r, F, R, W, C, n_s, n_tmp, factor = dims
    n_bits = n_r.bit_length() - 1
    SH = shard.shape[0]
    half = SH // 2
    CH = 4 if R % 4 == 0 else 1
    per = R // CH
    t, r = lax.axis_index("tm"), lax.axis_index("rows")
    bit = [lax.rem(lax.div(r, 1 << b), 2) for b in range(n_bits)]
    partner = [r + (1 - 2 * bit[b]) * (1 << b) for b in range(n_bits)]

    barrier = pltpu.get_barrier_semaphore()
    peers = [(lax.rem(t + k, n_t), r) for k in range(1, n_t)]
    peers += [(t, partner[b]) for b in range(n_bits)]
    peers += [(t, lax.rem(r + 1, n_r)), (t, lax.rem(r + n_r - 1, n_r))]
    for peer in peers:
        pl.semaphore_signal(barrier, inc=1, device_id=peer, device_id_type=MESH)
    pl.semaphore_wait(barrier, len(peers))

    def remote(src, dst, send, recv, peer):
        return pltpu.make_async_remote_copy(
            src_ref=src, dst_ref=dst, send_sem=send, recv_sem=recv, device_id=peer, device_id_type=MESH
        )

    own = tuple(bit[b] for b in reversed(range(n_bits)))
    gather[(t,) + own] = shard[...]
    ag_z = []
    for k in range(1, n_t):
        spot = gather.at[(t,) + own]
        ag_z.append(remote(spot, spot, ag_z_send.at[k - 1], ag_z_recv.at[k - 1], (lax.rem(t + k, n_t), r)))
        ag_z[-1].start()
    cot_in = pltpu.make_async_copy(cot_hbm, cot.at[pl.ds(0, F)], cot_sem)
    cot_in.start()

    def spread(values, f, row):
        col = lax.broadcasted_iota(jnp.int32, (W, C), 0)
        left = jnp.where(col == 0, 0.0, pltpu.roll(values, 1, 0))
        right = jnp.where(col == W - 1, 0.0, pltpu.roll(values, W - 1, 0))
        wide[f, row, :, 0:C] = left.astype(bf16)
        wide[f, row, :, C : 2 * C] = values.astype(bf16)
        wide[f, row, :, 2 * C : 3 * C] = right.astype(bf16)

    def act_row(f, h):
        normed, _ = normalize(video[f, h].astype(f32))
        act = normed * jax.nn.sigmoid(normed)
        spread(act, f, h + 1)
        act_t[f, :, pl.ds(pl.multiple_of(h * W, W), W)] = act.T.astype(bf16)

    def exchange(which):
        @pl.loop(0, F)
        def _(f):
            edge_out[2 * which, f] = wide[f, 1, :, C : 2 * C]
            edge_out[2 * which + 1, f] = wide[f, R, :, C : 2 * C]

        up = remote(
            edge_out.at[2 * which], edge_in.at[2 * which + 1],
            edge_send.at[2 * which], edge_recv.at[2 * which + 1], (t, r - 1),
        )
        down = remote(
            edge_out.at[2 * which + 1], edge_in.at[2 * which],
            edge_send.at[2 * which + 1], edge_recv.at[2 * which], (t, r + 1),
        )

        @pl.when(r > 0)
        def _():
            up.start()

        @pl.when(r < n_r - 1)
        def _():
            down.start()

        return up, down

    def receive(which, up, down):
        def fill(side, row):
            @pl.loop(0, F)
            def _(f):
                spread(edge_in[2 * which + side, f].astype(f32), f, row)

        def blank(row):
            @pl.loop(0, F)
            def _(f):
                wide[f, row] = jnp.zeros((W, 3 * C), bf16)

        @pl.when(r > 0)
        def _():
            up.wait_send()
            down.wait_recv()
            fill(0, 0)

        @pl.when(r == 0)
        def _():
            blank(0)

        @pl.when(r < n_r - 1)
        def _():
            down.wait_send()
            up.wait_recv()
            fill(1, R + 1)

        @pl.when(r == n_r - 1)
        def _():
            blank(R + 1)

    @pl.loop(0, F)
    def _(f):
        act_row(f, 0)
        act_row(f, R - 1)

    up_a, down_a = exchange(0)

    high = list(reversed(range(n_bits)))
    swapped = [high[1], high[0]] + high[2:] if n_bits >= 3 else high
    streams = [(high, 0), (swapped, half)]

    def ag_step(step):
        copies = []
        for s, (order, start) in enumerate(streams):
            done = order[:step]
            index = tuple(slice(None) if b in done else bit[b] for b in high)
            spot = gather.at[(slice(None),) + index + (pl.ds(start, half),)]
            b = order[step]
            copies.append(remote(spot, spot, ag_send.at[s, step], ag_recv.at[s, step], (t, partner[b])))
        for copy in copies:
            copy.start()
        return copies

    def finish(copies):
        for copy in copies:
            copy.wait()

    finish(ag_z)
    going = ag_step(0)
    ahead = remote(cot_hbm.at[pl.ds(0, 2)], cot.at[pl.ds(F, 2)], frame_send.at[0], frame_recv.at[0], (t - 1, r))

    @pl.when(t > 0)
    def _():
        ahead.start()

    @pl.loop(0, F * (R - 2))
    def _(i):
        act_row(lax.div(i, R - 2), lax.rem(i, R - 2) + 1)

    finish(going)
    going = ag_step(1) if n_bits > 1 else []
    receive(0, up_a, down_a)
    finish(going)
    for step in range(2, n_bits):
        finish(ag_step(step))

    for d in range(n_t * n_r):
        rr = d % n_r
        piece = gather[(d // n_r,) + tuple((rr >> b) & 1 for b in high)].astype(f32)
        acc_s[d * n_s : (d + 1) * n_s] = piece[:n_s]
        acc_t[d * n_tmp : (d + 1) * n_tmp] = piece[n_s : n_s + n_tmp]
    w_s[...] = acc_s[...].astype(bf16)
    w_t[...] = acc_t[...].astype(bf16)

    def forward(i):
        f = F - 1 - lax.div(i, per)
        h = lax.rem(i, per) * CH
        total = jnp.zeros((CH * W, C), f32)
        for ky in range(3):
            total += mm(wide[f, pl.ds(h + ky, CH)].reshape(CH * W, 3 * C), w_s[3 * C * ky : 3 * C * (ky + 1)])
        sigmoid = jax.nn.sigmoid(total)
        slope[f, pl.ds(h, CH)] = (sigmoid * (1.0 + total * (1.0 - sigmoid))).reshape(CH, W, C)
        hidden = total * sigmoid
        hid[f + 2, pl.ds(h, CH)] = hidden.astype(bf16).reshape(CH, W, C)
        hid_t[f, :, pl.ds(pl.multiple_of(h * W, W), CH * W)] = hidden.T.astype(bf16)

    pl.loop(0, 2 * per)(forward)
    past = remote(hid.at[pl.ds(F, 2)], hid.at[pl.ds(0, 2)], frame_send.at[1], frame_recv.at[1], (t + 1, r))

    @pl.when(t < n_t - 1)
    def _():
        past.start()

    pl.loop(2 * per, F * per)(forward)

    for i in range(3):
        for j in range(3):
            source = C * (3 * (2 - i) + 2 - j)
            wb_s[C * (3 * i + j) : C * (3 * i + j + 1)] = acc_s[source : source + C].T.astype(bf16)
        wb_t[C * i : C * (i + 1)] = acc_t[C * (2 - i) : C * (3 - i)].T.astype(bf16)

    cot_in.wait()

    @pl.when(t > 0)
    def _():
        ahead.wait_send()

    @pl.when(t < n_t - 1)
    def _():
        ahead.wait_recv()

    @pl.when(t == n_t - 1)
    def _():
        cot[F : F + 2] = jnp.zeros((2, R, W, C), bf16)

    def back(i):
        f = lax.div(i, per)
        h = lax.rem(i, per) * CH
        total = jnp.zeros((CH * W, C), f32)
        for m in range(3):
            total += mm(cot[f + m, pl.ds(h, CH)].reshape(CH * W, C), wb_t[C * m : C * (m + 1)])
        for k in range(CH):
            spread(total[k * W : (k + 1) * W] * slope[f, h + k], f, h + k + 1)

    pl.loop(0, F * per)(back)
    up_g, down_g = exchange(1)

    for k in range(3):
        acc_t[C * k : C * (k + 1)] = jnp.zeros((C, C), f32)

    @pl.loop(0, F)
    def _(f):
        for k in range(3):
            acc_t[C * k : C * (k + 1)] += mm(hid_t[f], cot[f + 2 - k].reshape(R * W, C))

    def mix(i):
        f = lax.div(i, per)
        h = lax.rem(i, per) * CH
        total = video[f, pl.ds(h, CH)].reshape(CH * W, C).astype(f32)
        for k in range(3):
            total += mm(hid[f + k, pl.ds(h, CH)].reshape(CH * W, C), w_t[C * k : C * (k + 1)])
        output[f, pl.ds(h, CH)] = total.astype(bf16).reshape(CH, W, C)

    pl.loop(2 * per, F * per)(mix)
    receive(1, up_g, down_g)

    acc_s[...] = jnp.zeros(acc_s.shape, f32)

    @pl.loop(0, F)
    def _(f):
        for i in range(3):
            found = mm(act_t[f], wide[f, pl.ds(i, R)].reshape(R * W, 3 * C))
            for j in range(3):
                block = C * (3 * (2 - i) + 2 - j)
                acc_s[block : block + C] += found[:, C * j : C * (j + 1)]

    for d in range(n_t * n_r):
        work[d, :n_s] = acc_s[d * n_s : (d + 1) * n_s]
        work[d, n_s : n_s + n_tmp] = acc_t[d * n_tmp : (d + 1) * n_tmp]
        if n_s + n_tmp < SH:
            work[d, n_s + n_tmp :] = jnp.zeros((SH - n_s - n_tmp, C), f32)

    offsets = []
    place = 0
    for b in range(n_bits):
        offsets.append(place)
        place += n_t * (1 << (n_bits - 1 - b))

    def slot(b, s, mine):
        count = 1 << (n_bits - 1 - b)
        tt, hi = lax.div(s, count), lax.rem(s, count)
        low = lax.rem(r, 1 << b)
        this = bit[b] if mine else 1 - bit[b]
        return tt * n_r + hi * (1 << (b + 1)) + this * (1 << b) + low

    def rs_start(b):
        count = n_t * (1 << (n_bits - 1 - b))

        @pl.loop(0, count)
        def _(s):
            rs_out[offsets[b] + s] = work[slot(b, s, False)].astype(bf16)

        span = pl.ds(offsets[b], count)
        copy = remote(rs_out.at[span], rs_in.at[span], rs_send.at[b], rs_recv.at[b], (t, partner[b]))
        copy.start()
        return copy

    def rs_finish(b, copy):
        copy.wait()

        @pl.loop(0, n_t * (1 << (n_bits - 1 - b)))
        def _(s):
            spot = slot(b, s, True)
            work[spot] = work[spot] + rs_in[offsets[b] + s].astype(f32)

    def data_back(i):
        f = lax.div(i, per)
        h = lax.rem(i, per) * CH
        total = jnp.zeros((CH * W, C), f32)
        for k in range(3):
            total += mm(wide[f, pl.ds(h + k, CH)].reshape(CH * W, 3 * C), wb_s[3 * C * k : 3 * C * (k + 1)])
        for k in range(CH):
            normed, inv_rms = normalize(video[f, h + k].astype(f32))
            grad_norm = total[k * W : (k + 1) * W] * silu_slope(normed)
            grad_in = inv_rms * (grad_norm - normed * jnp.mean(grad_norm * normed, axis=-1, keepdims=True))
            grad_video[f, h + k] = (cot[f, h + k].astype(f32) + grad_in).astype(bf16)

    chunks = F * per
    going = rs_start(0)
    for b in range(n_bits):
        pl.loop(b * chunks // n_bits, (b + 1) * chunks // n_bits)(data_back)
        rs_finish(b, going)
        if b + 1 < n_bits:
            going = rs_start(b + 1)

    z_copies = []
    for k in range(1, n_t):
        to = lax.rem(t + k, n_t)
        z_out[k - 1] = work[to * n_r + r].astype(bf16)
        z_copies.append(
            remote(z_out.at[k - 1], z_in.at[k - 1], z_send.at[k - 1], z_recv.at[k - 1], (to, r))
        )
        z_copies[-1].start()

    @pl.when(t < n_t - 1)
    def _():
        past.wait_send()

    @pl.when(t > 0)
    def _():
        past.wait_recv()

    @pl.when(t == 0)
    def _():
        hid[0:2] = jnp.zeros((2, R, W, C), bf16)

    pl.loop(0, 2 * per)(mix)

    finish(z_copies)
    total = work[t * n_r + r]
    for k in range(n_t - 1):
        total += z_in[k].astype(f32)
    grads[...] = total * factor


def shards(video, spatial_weight, temporal_weight, cotangent):
    _, F, R, W, C = video.shape
    n_t, n_r = lax.axis_size("tm"), lax.axis_size("rows")
    n_s, n_tmp = spatial_weight.shape[0], temporal_weight.shape[0]
    SH = -(-(n_s + n_tmp) // 32) * 32
    n_bits = n_r.bit_length() - 1
    total_cells = F * R * W * n_t * n_r
    factor = float(total_cells) ** (-0.5)
    parts = [spatial_weight, temporal_weight]
    if SH > n_s + n_tmp:
        parts.append(jnp.zeros((SH - n_s - n_tmp, C), bf16))
    shard = jnp.concatenate(parts, axis=0)
    dims = (n_t, n_r, F, R, W, C, n_s, n_tmp, factor)
    n_all = n_t * n_r
    rs_slots = n_t * (n_r - 1)
    dma = pltpu.SemaphoreType.DMA
    vmem = pl.BlockSpec(memory_space=pltpu.VMEM)
    output, grad_video, grads = pl.pallas_call(
        functools.partial(kernel, dims),
        out_shape=(
            jax.ShapeDtypeStruct((F, R, W, C), bf16),
            jax.ShapeDtypeStruct((F, R, W, C), bf16),
            jax.ShapeDtypeStruct((SH, C), f32),
        ),
        in_specs=[vmem, vmem, pl.BlockSpec(memory_space=pl.ANY)],
        out_specs=(vmem, vmem, vmem),
        scratch_shapes=[
            pltpu.VMEM((F, R + 2, W, 3 * C), bf16),
            pltpu.VMEM((F, C, R * W), bf16),
            pltpu.VMEM((F, R, W, C), f32),
            pltpu.VMEM((F + 2, R, W, C), bf16),
            pltpu.VMEM((F, C, R * W), bf16),
            pltpu.VMEM((F + 2, R, W, C), bf16),
            pltpu.VMEM((n_s * n_all, C), f32),
            pltpu.VMEM((n_tmp * n_all, C), f32),
            pltpu.VMEM((n_all, SH, C), f32),
            pltpu.VMEM((n_s * n_all, C), bf16),
            pltpu.VMEM((n_tmp * n_all, C), bf16),
            pltpu.VMEM((n_s * n_all, C), bf16),
            pltpu.VMEM((n_tmp * n_all, C), bf16),
            pltpu.VMEM((n_t,) + (2,) * n_bits + (SH, C), bf16),
            pltpu.VMEM((4, F, W, C), bf16),
            pltpu.VMEM((4, F, W, C), bf16),
            pltpu.VMEM((rs_slots, SH, C), bf16),
            pltpu.VMEM((rs_slots, SH, C), bf16),
            pltpu.VMEM((n_t - 1, SH, C), bf16),
            pltpu.VMEM((n_t - 1, SH, C), bf16),
            dma((n_t - 1,)), dma((n_t - 1,)),
            dma((2, n_bits)), dma((2, n_bits)),
            dma((4,)), dma((4,)),
            dma((2,)), dma((2,)),
            dma((n_bits,)), dma((n_bits,)),
            dma((n_t - 1,)), dma((n_t - 1,)),
            dma,
        ],
        compiler_params=pltpu.CompilerParams(
            collective_id=0, has_side_effects=True, vmem_limit_bytes=58 * 1024 * 1024
        ),
        cost_estimate=pl.CostEstimate(
            flops=24 * F * R * W * C * C * 3, bytes_accessed=F * R * W * C * 8, transcendentals=F * R * W * C * 3
        ),
    )(video[0], shard, cotangent[0])
    return (output[None], grad_video[None], grads[:n_s], grads[n_s : n_s + n_tmp])


def solution(mesh):
    in_specs = (
        P(None, "tm", "rows", None, None),
        P(("tm", "rows"), None),
        P(("tm", "rows"), None),
        P(None, "tm", "rows", None, None),
    )
    out_specs = (
        P(None, "tm", "rows", None, None),
        P(None, "tm", "rows", None, None),
        P(("tm", "rows"), None),
        P(("tm", "rows"), None),
    )
    return jax.shard_map(shards, mesh=mesh, in_specs=in_specs, out_specs=out_specs, check_vma=False)
```

time: 306 us -> 85.6 us (0.28)
  waiting for transfers between devices: 114 us -> 0 us
  Pallas kernels: 0 us -> 75.7 us
  blocking collectives: 62.7 us -> 0 us
  matrix products: 44.7 us -> 0 us
  other arithmetic: 26.1 us -> 1.41 us
  local copies, waits for them, and re-layouts: 31.1 us -> 7.47 us
  between operations: 14.3 us -> 0.64 us
  starting transfers between devices: 12.2 us -> 0 us
    reduce_scatter x4 -> x0, waiting for transfers between devices: 109 us -> none  [the longest x1 42 us: shards(): lax.psum_scatter(grad_spatial, 'tm', scatter_dimension=0, tiled=True)]
    pallas_call x0 -> x1, Pallas kernels: none -> 75.7 us  [shards(): pl.pallas_call(functools.partial(kernel, dims), out_shape=(jax.ShapeDtype...]
    all_gather x1 -> x0, blocking collectives: 62.7 us -> none  [shards(): lax.all_gather(temporal_weight, ('tm', 'rows'), axis=0, tiled=True)]
    dot_general x30 -> x0, matrix products: 44.7 us -> none  [the longest x10 20.4 us: contract(): lax.dot_general(left, right, (((0,), (0,)), ((), ())), preferred_element_...]
    slice x7 -> x2, local copies, waits for them, and re-layouts: 18.2 us -> 2.87 us  [shards(): return (output[None], grad_video[None], grads[:n_s], grads[n_s:n_s + n_tmp])]
    ppermute x6 -> x0, starting transfers between devices: 11.5 us -> none  [the longest x2 5.12 us: with_halo(): before = lax.ppermute(last, axis, up)]
    concatenate x5 -> x1, other arithmetic: 10.6 us -> 1.41 us  [shards(): shard = jnp.concatenate(parts, axis=0)]
    convert_element_type x3 -> x0, other arithmetic: 7.91 us -> none  [the longest x1 5.46 us: shards(): grad_video = (cotangent.astype(jnp.float32) + grad_in).astype(jnp.bfloat16)]
  transfers between devices with their start and end apart: 11 -> 0, of which waited for: 4 -> 0; matrix products, arithmetic and copies ran while one was open for 25% -> 0% of each run, Pallas kernels for 0% -> 0%
where the time goes in v1:
time: 85.6 us; the launch traced here: 85.2 us
  Pallas kernels  75.7 us (88%)
  local copies, waits for them, and re-layouts  7.47 us (9%)
  other arithmetic  1.41 us (2%)
    pallas_call x1, Pallas kernels, shards(): pl.pallas_call(functools.partial(kernel, dims), out_shape=(jax.ShapeDtype...  75.7 us
    unnamed x4, local copies, waits for them, and re-layouts  4.6 us
    slice x2, local copies, waits for them, and re-layouts, shards(): return (output[None], grad_video[None], grads[:n_s], grads[n_s:n_s + n_tmp])  2.87 us

profile of v1, /device:TPU:0, one launch (start us, length us, event | category | flops | bytes accessed | tf_op | source)
XLA Modules:
  0.0 85.2 jit_solution(17681430298679914223)
XLA Ops:
  0.6 1.4 %pad_maximum_fusion.shard = bf16[96,256]{1,0:T(8,128)(2,1)} fusion(bf16[24,256]{1,0:T(8,128)(2,1)} %param.6, bf16[72,256]{1,0:T(8,128)(2,1)} %param.5), kind=kLoop, calls=%fused_computation | loop fusion | flops 98304 | bytes 98304 | tf_op jit(solution)/shard_map/concatenate | solution.py:376
  2.0 75.7 %shard_map.75 = (bf16[4,8,128,256]{3,2,1,0:T(8,128)(2,1)}, bf16[4,8,128,256]{3,2,1,0:T(8,128)(2,1)}, f32[96,256]{1,0:T(8,128)}) custom-call(bf16[4,8,128,256]{3,2,1,0:T(8,128)(2,1)} %bitcast.6, bf16[96,256]{1,0:T(8,128)(2,1)} %pad_maximum_fusion.shard, bf16[4,8,128,256]{3,2,1,0:T(8,128)(2,1)} %bitcast.7), custom_call_target="tpu_custom_call" | custom-call | flops 19327352832 | bytes 8388608 | tf_op jit(solution)/shard_map/pallas_call | solution.py:382
  77.8 1.3 %slice.7 = f32[24,256]{1,0:T(8,128)} slice(f32[96,256]{1,0:T(8,128)} %get-tuple-element.9), slice={[72:96], [0:256]} | slice | bytes 49152 | tf_op jit(solution)/shard_map/slice | solution.py:427
  79.1 1.5 %slice.6 = f32[72,256]{1,0:T(8,128)} slice(f32[96,256]{1,0:T(8,128)} %get-tuple-element.9), slice={[0:72], [0:256]} | slice | bytes 147456 | tf_op jit(solution)/shard_map/slice | solution.py:427
  80.6 0.0 copy-start
  80.6 3.3 %copy.10 = bf16[1,4,8,128,256]{4,3,2,1,0:T(8,128)(2,1)} copy(bf16[1,4,8,128,256]{4,3,2,1,0:T(8,128)(2,1)} %bitcast.5) | data formatting | bytes 4194304
  83.9 0.0 copy-done
  83.9 1.3 %copy.11 = bf16[1,4,8,128,256]{4,3,2,1,0:T(8,128)(2,1)} copy(bf16[1,4,8,128,256]{4,3,2,1,0:T(8,128)(2,1)S(1)} %bitcast.4) | data formatting | bytes 4194304
Async XLA Ops:
  80.6 3.3 %copy-start = (bf16[4,8,128,256]{3,2,1,0:T(8,128)(2,1)S(1)}, bf16[4,8,128,256]{3,2,1,0:T(8,128)(2,1)}, u32[]{:S(2)}) copy-start(bf16[4,8,128,256]{3,2,1,0:T(8,128)(2,1)} %get-tuple-element.8) | copy-start | bytes 6291460
